TPU v7x, 256 devices: a whole 4x4x8 slice. The times are simulated.
256 devices in a mesh: row: 16 (over x_hi, z), col: 16 (over x_lo, y, core).
Axes of the slice: x: 4 (x_hi: 2, x_lo: 2; x = x_hi * 2 + x_lo), y: 4, z: 8, core: 2. Of those that a mesh axis runs over, the one named last changes fastest.
Arguments:
- features: bfloat16 [65536, 256], P(('col', 'row')), may hold values from -6 to 6
- block_values: bfloat16 [16, 16, 32, 128, 128], P('row', 'col'), may hold values from -0.25 to 0.25
- block_rows: int32 [16, 16, 32], P('row', 'col'), may hold values from 0 to 31, as said below
- block_cols: int32 [16, 16, 32], P('row', 'col'), may hold values from 0 to 31
- block_count: int32 [16, 16], P('row', 'col'), may hold values from 2 to 32, as said below
- weight_in: bfloat16 [256, 1024], replicated, may hold values from -0.375 to 0.375
- weight_out: bfloat16 [1024, 256], replicated, may hold values from -0.1875 to 0.1875
- cotangent: bfloat16 [65536, 256], P(('row', 'col')), may hold values from -6 to 6
Outputs:
- layer_out: bfloat16 [65536, 256], P(('row', 'col'))
- grad_x: bfloat16 [65536, 256], P(('col', 'row'))
- grad_w_in: float32 [256, 1024], replicated
- grad_w_out: float32 [1024, 256], replicated
Inputs may be any that keep to these rules, and one draw needn't show every extreme that they name: Within one device the slots name distinct blocks (pairs of block_rows and block_cols), live or not. `block_count`: one grid row, drawn from the seed, has 32 live slots on every device.
All inputs are finite; a program needn't handle non-finite values.
Results may differ from a plain program's by a relative error of at most 0.01.
Values may be sent and summed in bfloat16 or wider, within the bound.
A program may use at most 64 MiB of HBM per device.

v0:
```python
from functools import partial

import jax
import jax.numpy as jnp
from jax import lax
from jax.sharding import PartitionSpec as P

BLK = 128


def aggregate(values, target, source, live_mask, features, out_blocks, base, transpose):
    width = features.shape[1]
    taken = features.reshape(-1, BLK, width)[source]
    if transpose:
        prod = jnp.einsum("sji,sjf->sif", values, taken, preferred_element_type=jnp.float32)
    else:
        prod = jnp.einsum("sij,sjf->sif", values, taken, preferred_element_type=jnp.float32)
    relative = target - base
    inside = ((relative >= 0) & (relative < out_blocks)).astype(jnp.float32)
    prod = prod * (live_mask * inside)[:, None, None]
    placed = jnp.clip(relative, 0, out_blocks - 1)
    return jax.ops.segment_sum(prod, placed, num_segments=out_blocks).reshape(
        out_blocks * BLK, width
    )


def accumulate(values, target, source, live_mask, features, out_blocks, base, transpose):
    return aggregate(values, target, source, live_mask, features, out_blocks, base, transpose)


def body(
    features, block_values, block_rows, block_cols, block_count, weight_in, weight_out, cotangent
):
    values = block_values[0, 0]
    row_index = block_rows[0, 0]
    col_index = block_cols[0, 0]
    count = block_count[0, 0]
    slots = values.shape[0]
    live_mask = (jnp.arange(slots, dtype=jnp.int32) < count).astype(jnp.float32)
    gathered = lax.all_gather(features, "row", axis=0, tiled=True)
    own_rows = features.shape[0]
    row_blocks = own_rows * lax.axis_size("col") // BLK
    col_blocks = gathered.shape[0] // BLK
    partial_sum = accumulate(
        values, row_index, col_index, live_mask, gathered, row_blocks, 0, False
    )
    pooled = lax.psum_scatter(partial_sum, "col", scatter_dimension=0, tiled=True).astype(
        jnp.bfloat16
    )
    pre_act = jnp.dot(pooled, weight_in, preferred_element_type=jnp.float32)
    gelu_fn = partial(jax.nn.gelu, approximate=True)
    activated = gelu_fn(pre_act).astype(jnp.bfloat16)
    layer_out = (
        pooled.astype(jnp.float32)
        + jnp.dot(activated, weight_out, preferred_element_type=jnp.float32)
    ).astype(jnp.bfloat16)
    local_w_out = jnp.dot(activated.T, cotangent, preferred_element_type=jnp.float32)
    grad_act = jnp.dot(cotangent, weight_out.T, preferred_element_type=jnp.float32)
    grad_pre = jax.vjp(gelu_fn, pre_act)[1](grad_act)[0].astype(jnp.bfloat16)
    grad_pooled = (
        cotangent.astype(jnp.float32)
        + jnp.dot(grad_pre, weight_in.T, preferred_element_type=jnp.float32)
    ).astype(jnp.bfloat16)
    local_w_in = jnp.dot(pooled.T, grad_pre, preferred_element_type=jnp.float32)
    gathered_grad = lax.all_gather(grad_pooled, "col", axis=0, tiled=True)
    partial_back = accumulate(
        values, col_index, row_index, live_mask, gathered_grad, col_blocks, 0, True
    )
    grad_x = lax.psum_scatter(partial_back, "row", scatter_dimension=0, tiled=True).astype(
        jnp.bfloat16
    )
    grad_w_in, grad_w_out = lax.psum((local_w_in, local_w_out), ("row", "col"))
    return (layer_out, grad_x, grad_w_in, grad_w_out)


def solution(mesh):
    return jax.shard_map(
        body,
        mesh=mesh,
        in_specs=(
            P(("col", "row"), None),
            P("row", "col", None, None, None),
            P("row", "col", None),
            P("row", "col", None),
            P("row", "col"),
            P(),
            P(),
            P(("row", "col"), None),
        ),
        out_specs=(P(("row", "col"), None), P(("col", "row"), None), P(), P()),
        check_vma=False,
    )
```

profile of v0, /device:TPU:2, one launch (start us, length us, event | category | flops | bytes accessed | tf_op | source)
XLA Modules:
  0.0 738.1 jit_solution(9765829195830572567)
XLA Ops:
  7.2 0.0 copy-start
  7.2 0.0 all-gather.3.cloned.1.call-start
  7.2 0.7 all-gather.3.cloned.1.call-update
  7.9 0.0 reduce-scatter.3.cloned.1.call-start
  8.6 0.7 fusion.13
  9.3 0.7 bitcast_select_fusion.1
  9.9 0.7 fusion.12
  10.6 87.6 %all-gather.3.cloned.1.call-done = bf16[4096,256]{1,0:T(8,128)(2,1)} async-done(((bf16[256,256]{1,0:T(8,128)(2,1)}), bf16[4096,256]{1,0:T(8,128)(2,1)}) %all-gather.3.cloned.1.call-update) | async-done | bytes 2097168 | tf_op jit(solution)/shard_map/all_gather | solution.py:40
  98.2 2.3 gather_fusion
  100.5 0.0 copy-done
  100.5 2.9 multiply_bitcast_fusion.1
  103.4 5.6 copy.15
  109.0 2.5 broadcast.121.clone
  111.5 10.0 %scatter_fusion = f32[32,128,256]{2,1,0:T(8,128)} fusion(f32[32,128,256]{2,1,0:T(8,128)} %broadcast.121.clone, s32[32]{0:T(128)S(1)} %get-tuple-element.7, f32[32,128,256]{2,1,0:T(8,128)} %copy.15), kind=kCustom, calls=%fused_computation.2 | custom fusion | flops 1048576 | bytes 12583040 | tf_op jit(solution)/shard_map/scatter-add | solution.py:22
  121.5 0.0 copy-start.4
  121.5 0.0 copy-start.6
  121.5 0.0 copy-start.3
  121.5 0.0 reduce-scatter.3.cloned.1.call-update
  121.5 0.0 all-gather.5.cloned.1.call-start
  121.5 1.0 copy-done.4
  122.5 0.0 copy-done.6
  122.5 0.3 fusion.20
  122.9 0.0 copy-start.8
  122.9 64.6 %reduce-scatter.3.cloned.1.call-done = f32[256,256]{1,0:T(8,128)} async-done(((f32[4096,256]{1,0:T(8,128)}), f32[256,256]{1,0:T(8,128)}) %reduce-scatter.3.cloned.1.call-update) | async-done | bytes 262160 | tf_op jit(solution)/shard_map/reduce_scatter | solution.py:47
  187.4 0.0 copy-done.3
  187.4 2.7 fusion.8
  190.2 0.0 copy-start.1
  190.2 0.8 copy-done.1
  190.9 1.0 fusion.1
  191.9 0.0 all-gather.5.cloned.1.call-update
  192.0 0.0 reduce-scatter.5.cloned.1.call-start
  192.0 0.0 copy-done.8
  192.1 35.7 %all-gather.5.cloned.1.call-done = bf16[4096,256]{1,0:T(8,128)(2,1)} async-done(((bf16[256,256]{1,0:T(8,128)(2,1)}), bf16[4096,256]{1,0:T(8,128)(2,1)}) %all-gather.5.cloned.1.call-update) | async-done | bytes 2097168 | tf_op jit(solution)/shard_map/all_gather | solution.py:65
  227.8 2.3 gather_fusion.1
  230.0 2.9 multiply_bitcast_fusion
  233.0 5.6 copy.17
  238.6 2.5 broadcast.121
  241.0 10.0 %scatter_fusion.1 = f32[32,128,256]{2,1,0:T(8,128)} fusion(f32[32,128,256]{2,1,0:T(8,128)} %broadcast.121, s32[32]{0:T(128)S(1)} %get-tuple-element.8, f32[32,128,256]{2,1,0:T(8,128)} %copy.17), kind=kCustom, calls=%fused_computation.3 | custom fusion | flops 1048576 | bytes 12583040 | tf_op jit(solution)/shard_map/scatter-add | solution.py:22
  251.1 0.0 copy-start.2
  251.1 0.0 copy-start.7
  251.1 0.0 reduce-scatter.5.cloned.1.call-update
  251.1 0.0 copy-start.5
  251.1 0.0 all-reduce.3.cloned.1.call-start
  251.2 1.0 copy-done.2
  252.1 0.1 copy-done.7
  252.2 1.3 fusion.15
  253.5 2.8 fusion.19
  256.3 0.0 all-reduce.3.cloned.1.call-update
  256.3 0.0 copy-done.5
  256.3 2.4 fusion
  258.7 200.6 %reduce-scatter.5.cloned.1.call-done = f32[256,256]{1,0:T(8,128)} async-done(((f32[4096,256]{1,0:T(8,128)}), f32[256,256]{1,0:T(8,128)}) %reduce-scatter.5.cloned.1.call-update) | async-done | bytes 262160 | tf_op jit(solution)/shard_map/reduce_scatter | solution.py:69
  459.3 1.6 convert_element_type.44
  460.9 266.1 %all-reduce.3.cloned.1.call-done = (f32[256,1024]{1,0:T(8,128)}, f32[1024,256]{1,0:T(8,128)}) async-done(((f32[256,1024]{1,0:T(8,128)}, f32[1024,256]{1,0:T(8,128)}), (f32[256,1024]{1,0:T(8,128)}, f32[1024,256]{1,0:T(8,128)})) %all-reduce.3.cloned.1.call-update) | async-done | bytes 2097168 | tf_op jit(solution)/shard_map/psum | solution.py:72
  727.0 2.3 copy.25
  729.3 2.3 copy.26
  (3 shorter events, 0.0 us)
Async XLA Ops:
  7.2 93.3 %copy-start = (bf16[1,1,32,128,128]{4,3,2,1,0:T(8,128)(2,1)S(1)}, bf16[1,1,32,128,128]{4,3,2,1,0:T(8,128)(2,1)}, u32[]{:S(2)}) copy-start(bf16[1,1,32,128,128]{4,3,2,1,0:T(8,128)(2,1)} %param.9) | copy-start | bytes 3145732
  7.2 91.0 %all-gather.3.cloned.1.call-start = ((), (), s32[]{:S(2)}) async-start(), calls=%async_computation.2 | async-start | bytes 2228224 | tf_op jit(solution)/shard_map/all_gather | solution.py:40
  7.9 179.5 %reduce-scatter.3.cloned.1.call-start = ((), (), s32[]{:S(2)}) async-start(), calls=%async_computation.3 | async-start | bytes 4456448 | tf_op jit(solution)/shard_map/reduce_scatter | solution.py:47
  121.5 1.0 copy-start.4
  121.5 1.1 copy-start.6
  121.5 66.0 %copy-start.3 = (bf16[256,1024]{1,0:T(8,128)(2,1)S(1)}, bf16[256,1024]{1,0:T(8,128)(2,1)}, u32[]{:S(2)}) copy-start(bf16[256,1024]{1,0:T(8,128)(2,1)} %param.13) | copy-start | bytes 1572868
  121.5 106.3 %all-gather.5.cloned.1.call-start = ((), (), s32[]{:S(2)}) async-start(), calls=%async_computation.4 | async-start | bytes 2228224 | tf_op jit(solution)/shard_map/all_gather | solution.py:65
  122.9 69.2 %copy-start.8 = (s32[1,1,32]{2,1,0:T(1,128)S(1)}, s32[1,1,32]{2,1,0:T(1,128)}, u32[]{:S(2)}) copy-start(s32[1,1,32]{2,1,0:T(1,128)} %param.11) | copy-start | bytes 388
  190.2 0.8 copy-start.1
  192.0 267.3 %reduce-scatter.5.cloned.1.call-start = ((), (), s32[]{:S(2)}) async-start(), calls=%async_computation.5 | async-start | bytes 4456448 | tf_op jit(solution)/shard_map/reduce_scatter | solution.py:69
  251.1 1.0 copy-start.2
  251.1 1.1 copy-start.7
  251.1 5.2 copy-start.5
  251.1 475.9 %all-reduce.3.cloned.1.call-start = ((), (), s32[]{:S(2)}) async-start(), calls=%async_computation.6 | async-start | bytes 4194304 | tf_op jit(solution)/shard_map/psum | solution.py:72
Sparse Core Ops, SparseCore 0:
  10.6 87.5 all-gather.2
  121.6 65.7 reduce-scatter.2
  192.1 35.6 all-gather.4
  251.2 207.9 reduce-scatter.4
  466.2 260.8 all-reduce.2
where the time goes:
time: 739 us; the launch traced here: 738 us
  waiting for transfers between devices  655 us (89%)
  local copies, waits for them, and re-layouts  28.1 us (4%)
  other arithmetic  23.6 us (3%)
  matrix products  16.3 us (2%)
  between operations  14.5 us (2%)
    psum x1, waiting for transfers between devices, body(): grad_w_in, grad_w_out = lax.psum((local_w_in, local_w_out), ('row', 'col'))  266 us
    reduce_scatter x1, waiting for transfers between devices, body(): lax.psum_scatter(partial_back, 'row', scatter_dimension=0, tiled=True)  201 us
    all_gather x1, waiting for transfers between devices, body(): gathered = lax.all_gather(features, 'row', axis=0, tiled=True)  87.6 us
    reduce_scatter x1, waiting for transfers between devices, body(): lax.psum_scatter(partial_sum, 'col', scatter_dimension=0, tiled=True)  64.6 us
    all_gather x1, waiting for transfers between devices, body(): gathered_grad = lax.all_gather(grad_pooled, 'col', axis=0, tiled=True)  35.7 us
    scatter-add x2, other arithmetic, aggregate(): jax.ops.segment_sum(prod, placed, num_segments=out_blocks)  20 us
  transfers between devices with their start and end apart: 5, of which 5 were waited for; matrix products, arithmetic and copies ran while one was open for 1% of the time, Pallas kernels for 0%

commit v1 on v0

v1 whole, which is shorter than its diff:
```python
import jax
import jax.numpy as jnp
from jax import lax
from jax.experimental import pallas as pl
from jax.experimental.pallas import tpu as pltpu
from jax.sharding import PartitionSpec as P

MESH = pl.DeviceIdType.MESH
F32, BF16 = jnp.float32, jnp.bfloat16
BLK, WIDTH, HID, SLOTS, BLOCKS = 128, 256, 1024, 32, 32
ROWS, COLS, PREV_F, PREV_B, LAST_F, LAST_B = range(6)


def dot(a, b, ca=1, cb=0):
    return lax.dot_general(a, b, (((ca,), (cb,)), ((), ())), preferred_element_type=F32)


def kernel(
    tab, count, feat, values_h, win_h, wout_h, cot_h,
    lout, gx, gwin, gwout,
    val, valt, win, wout, cot,
    feats, grads, scan, pstage, precv, qstage, qrecv, own,
    zstage, zrecv, xstage, xrecv, gpool,
    wacc, wstage, wrecv0, wsend1, wrecv1, wsum, wsend2, wrecv2, wsend3, wfull,
    sem_in, s_ag, r_ag, s_x, r_x, s_p, r_p, s_q, r_q, s_g, r_g, s_gf, r_gf,
    s_z, r_z, s_w, r_w, s_w1, r_w1, s_w2, r_w2, s_w3, r_w3, s_w4, r_w4, s_w5, r_w5,
):
    r, c = lax.axis_index("row"), lax.axis_index("col")
    xh, z = r // 8, r % 8
    j, k = c // 2, c % 2
    xl, y = j // 4, j % 4
    sibling = (r, 2 * j + 1 - k)

    def chip(m):
        return ((xl + m // 4) % 2) * 4 + (y + m % 4) % 4

    def behind(m):
        return ((xl + m // 4) % 2) * 4 + (y + 4 - m % 4) % 4

    def rank(n):
        return ((xh + n // 8) % 2) * 8 + (z + n % 8) % 8

    def remote(src, dst, ss, rs, to):
        return pltpu.make_async_remote_copy(
            src_ref=src, dst_ref=dst, send_sem=ss, recv_sem=rs, device_id=to, device_id_type=MESH
        )

    def each(lo, hi, f):
        lax.fori_loop(lo, hi, lambda i, _: (f(i), 0)[1], 0)

    loads = [
        pltpu.make_async_copy(a, b, sem_in.at[i])
        for i, (a, b) in enumerate(((values_h, val), (win_h, win), (wout_h, wout), (cot_h, cot)))
    ]
    for one in loads:
        one.start()

    barrier = pltpu.get_barrier_semaphore()
    pl.semaphore_signal(barrier, inc=1, device_id=sibling, device_id_type=MESH)
    each(1, 8, lambda m: pl.semaphore_signal(
        barrier, inc=1, device_id=(r, 2 * chip(m) + k), device_id_type=MESH))
    each(1, 16, lambda n: pl.semaphore_signal(
        barrier, inc=1, device_id=(rank(n), c), device_id_type=MESH))
    pl.semaphore_wait(barrier, 23)

    partner = ((1 - xh) * 8 + z, c)
    sign = (1, 7)
    ahead = [(xh * 8 + (z + g) % 8, c) for g in sign]

    def ag_copy(d, s, p):
        plane = (xh + p) % 2
        at = 2 * (plane * 8 + (z + (8 - sign[d]) * s) % 8)
        part = pl.ds(at, 2) if s < 3 else pl.ds(at + d, 1)
        src = feat if s == 0 and p == 0 else feats.at[part]
        return remote(src, feats.at[part], s_ag.at[d, s, p], r_ag.at[d, s, p], ahead[d])

    swap = remote(feat, feats.at[pl.ds(2 * r, 2)], s_x.at[0], r_x.at[0], partner)
    for d in (0, 1):
        ag_copy(d, 0, 0).start()
    swap.start()
    feats[pl.ds(2 * r, 2)] = feat[...]

    loads[0].wait()

    def mask(s):
        live = jnp.where(s < count[0], 1.0, 0.0).astype(F32)
        masked = val[s].astype(F32) * live
        val[s] = masked.astype(BF16)
        valt[s] = masked.T.astype(BF16)

    for s in range(4):
        for p in (0, 1):
            if s == 0 and p == 0:
                continue
            if s == 0:
                swap.wait_recv()
            for d in (0, 1):
                if s > 0:
                    ag_copy(d, s - 1, p).wait_recv()
                ag_copy(d, s, p).start()
        each(8 * s, 8 * s + 8, mask)
    for one in loads[1:]:
        one.wait()
    for d in (0, 1):
        for p in (0, 1):
            ag_copy(d, 3, p).wait_recv()

    def aggregate(vals, source, prev, data):
        scan[0] = jnp.zeros((BLK, WIDTH), F32)

        def some(g):
            for u in range(8):
                s = g * 8 + u
                scan[s + 1] = dot(vals[s], data[tab[source, s]]) + scan[tab[prev, s]]

        each(0, SLOTS // 8, some)

    aggregate(val, COLS, PREV_F, feats)

    def p_copy(m):
        return remote(pstage.at[m], precv.at[m], s_p.at[m], r_p.at[m], sibling)

    def q_copy(m):
        return remote(
            qstage.at[m], qrecv.at[m], s_q.at[m], r_q.at[m], (r, 2 * chip(m) + k))

    def give(i):
        m = (i + 1) % 8
        at = 2 * (2 * chip(m) + 1 - k)
        for h in (0, 1):
            pstage[m, h] = scan[tab[LAST_F, at + h]].astype(BF16)
        p_copy(m).start()

    each(0, 8, give)

    def pair_sum(m, h):
        return scan[tab[LAST_F, 2 * (2 * chip(m) + k) + h]] + precv[m, h].astype(F32)

    def spread(m):
        p_copy(m).wait_recv()
        for h in (0, 1):
            qstage[m, h] = pair_sum(m, h).astype(BF16)
        q_copy(m).start()

    each(1, 8, spread)
    p_copy(0).wait_recv()
    for h in (0, 1):
        own[h] = pair_sum(0, h)

    def collect(m):
        q_copy(m).wait_recv()
        for h in (0, 1):
            own[h] += qrecv[m, h].astype(F32)

    each(1, 8, collect)

    pooled = own[...].reshape(2 * BLK, WIDTH).astype(BF16)
    ct = cot[...]
    out = pooled.astype(F32)
    back = ct.astype(F32)
    a0, a1 = 0.7978845608028654, 0.044715
    for t in range(4):
        cut = pl.ds(t * 256, 256)
        w_in, w_out = win[:, cut], wout[cut, :]
        pre = dot(pooled, w_in)
        square = pre * pre
        th = jnp.tanh(a0 * (pre + a1 * (square * pre)))
        cdf = 0.5 * (1.0 + th)
        act = (pre * cdf).astype(BF16)
        slope = cdf + 0.5 * pre * (1.0 - th * th) * (a0 * (1.0 + 3.0 * a1 * square))
        gpre = (dot(ct, w_out, 1, 1) * slope).astype(BF16)
        out = out + dot(act, w_out)
        back = back + dot(gpre, w_in, 1, 1)
        g_out = dot(act, ct, 0, 0)
        g_in = dot(pooled, gpre, 0, 0)
        for h in (0, 1):
            wacc[pl.ds(h * 1024 + t * 256, 256), :] = g_out[:, h * 128:(h + 1) * 128]
            wacc[pl.ds(2048 + (2 * t + h) * 256, 256), :] = g_in[:, h * 128:(h + 1) * 128]
    lout[...] = out.astype(BF16)
    gpool[...] = back.astype(BF16).reshape(2, BLK, WIDTH)

    def g_copy(m):
        return remote(
            gpool, grads.at[pl.ds(2 * c, 2)], s_g.at[m], r_g.at[m], (r, 2 * chip(m) + k))

    def gf_copy(m):
        at = pl.ds(2 * (2 * behind(m) + k), 2)
        return remote(grads.at[at], grads.at[at], s_gf.at[m], r_gf.at[m], sibling)

    each(1, 8, lambda m: g_copy(m).start())
    grads[pl.ds(2 * c, 2)] = gpool[...]
    gf_copy(0).start()

    def wchunk(n):
        return wacc[pl.ds(256 * n, 256), :]

    def wgive(m):
        wstage[m] = wchunk(2 * chip(m) + 1 - k).astype(BF16)

    each(0, 8, wgive)
    w0 = remote(wstage, wrecv0, s_w.at[0], r_w.at[0], sibling)
    w0.start()

    def pass_on(m):
        g_copy(m).wait_recv()
        gf_copy(m).start()

    each(1, 8, pass_on)

    def w1_copy(m):
        return remote(
            wsend1.at[m], wrecv1.at[m], s_w1.at[m], r_w1.at[m], (r, 2 * chip(m) + k))

    w0.wait_recv()

    def wspread(m):
        wsend1[m] = (wchunk(2 * chip(m) + k) + wrecv0[m].astype(F32)).astype(BF16)
        w1_copy(m).start()

    each(1, 8, wspread)
    wsum[...] = wchunk(c) + wrecv0[0].astype(F32)

    each(0, 8, lambda m: gf_copy(m).wait_recv())
    aggregate(valt, ROWS, PREV_B, grads)

    def z_copy(d, s, p):
        part = pl.ds(0, 2) if s > 0 else pl.ds(d, 1)
        return remote(
            zstage.at[d, s, p, part], zrecv.at[d, s, p, part],
            s_z.at[d, s, p], r_z.at[d, s, p], ahead[d])

    def term(p, zz, h):
        return scan[tab[LAST_B, 2 * (((xh + p) % 2) * 8 + zz % 8) + h]]

    def z_step(s):
        for p in (1, 0):
            for d in (0, 1):
                target = z + sign[d] * (4 - s)
                if s > 0:
                    z_copy(d, s - 1, p).wait_recv()
                for h in (0, 1):
                    if s == 0 and h != d:
                        continue
                    v = term(p, target, h)
                    if s > 1 or (s == 1 and h == d):
                        v = v + zrecv[d, s - 1, p, h].astype(F32)
                    zstage[d, s, p, h] = v.astype(BF16)
                z_copy(d, s, p).start()

    z_step(0)

    def w2_copy(n):
        return remote(
            wsend2.at[rank(n)], wrecv2.at[n], s_w2.at[n], r_w2.at[n], (rank(n), c))

    def wcollect(m):
        w1_copy(m).wait_recv()
        wsum[...] += wrecv1[m].astype(F32)

    each(1, 8, wcollect)
    wsend2[...] = wsum[...].astype(BF16).reshape(16, 16, 128)
    each(1, 16, lambda n: w2_copy(n).start())

    z_step(1)

    place = pl.ds(pl.multiple_of(256 * c + 16 * r, 16), 16)

    def w3_copy(n):
        return remote(wsend3, wfull.at[place], s_w3.at[n], r_w3.at[n], (rank(n), c))

    def wadd(n, total):
        w2_copy(n).wait_recv()
        return total + wrecv2[n].astype(F32)

    piece = lax.fori_loop(1, 16, wadd, wsum[pl.ds(pl.multiple_of(16 * r, 16), 16), :])
    wsend3[...] = piece.astype(BF16)
    wfull[place, :] = wsend3[...]
    each(1, 16, lambda n: w3_copy(n).start())

    z_step(2)

    def chunk(n):
        return wfull.at[pl.ds(pl.multiple_of(256 * n, 256), 256)]

    def w4_copy(m):
        return remote(chunk(c), chunk(c), s_w4.at[m], r_w4.at[m], (r, 2 * chip(m) + k))

    def w5_copy(m):
        part = chunk(2 * behind(m) + k)
        return remote(part, part, s_w5.at[m], r_w5.at[m], sibling)

    each(1, 16, lambda n: w3_copy(n).wait_recv())
    each(1, 8, lambda m: w4_copy(m).start())
    w5_copy(0).start()

    z_step(3)

    def wpass(m):
        w4_copy(m).wait_recv()
        w5_copy(m).start()

    each(1, 8, wpass)

    def arrived(p, h):
        v = term(p, z, h)
        return v + zrecv[0, 3, p, h].astype(F32) + zrecv[1, 3, p, h].astype(F32)

    for d in (0, 1):
        z_copy(d, 3, 1).wait_recv()
    for h in (0, 1):
        xstage[h] = arrived(1, h).astype(BF16)
    last = remote(xstage, xrecv, s_x.at[1], r_x.at[1], partner)
    last.start()
    for d in (0, 1):
        z_copy(d, 3, 0).wait_recv()
    mine = [arrived(0, h) for h in (0, 1)]

    each(0, 8, lambda m: w5_copy(m).wait_recv())
    for h in (0, 1):
        gwout[:, h * 128:(h + 1) * 128] = wfull[pl.ds(h * 1024, 1024), :]
    for t in range(8):
        gwin[:, t * 128:(t + 1) * 128] = wfull[pl.ds(2048 + t * 256, 256), :]
    last.wait_recv()
    for h in (0, 1):
        gx[h] = (mine[h] + xrecv[h].astype(F32)).astype(BF16)

    swap.wait_send()
    last.wait_send()
    w0.wait_send()
    for d in (0, 1):
        for s in range(4):
            for p in (0, 1):
                ag_copy(d, s, p).wait_send()
                z_copy(d, s, p).wait_send()

    def drain(m):
        for f in (p_copy, gf_copy, w5_copy):
            f(m).wait_send()

    def drain_chips(m):
        for f in (q_copy, g_copy, w1_copy, w4_copy):
            f(m).wait_send()

    def drain_ranks(n):
        w2_copy(n).wait_send()
        w3_copy(n).wait_send()

    each(0, 8, drain)
    each(1, 8, drain_chips)
    each(1, 16, drain_ranks)


def tables(rows, cols):
    keys = jnp.stack([rows, cols])
    slot = jnp.arange(SLOTS, dtype=jnp.int32)
    same = keys[:, :, None] == keys[:, None, :]
    before = slot[None, :] < slot[:, None]
    prev = jnp.max(jnp.where(same & before, slot[None, None, :] + 1, 0), axis=2)
    block = jnp.arange(BLOCKS, dtype=jnp.int32)
    hit = keys[:, None, :] == block[None, :, None]
    last = jnp.max(jnp.where(hit, slot[None, None, :] + 1, 0), axis=2)
    return jnp.concatenate([keys, prev, last]).astype(jnp.int32)


def body(features, block_values, block_rows, block_cols, block_count, weight_in, weight_out, cot):
    tab = tables(block_rows[0, 0], block_cols[0, 0])
    vm = lambda *shape, t=BF16: pltpu.VMEM(shape, t)
    dma = lambda *shape: pltpu.SemaphoreType.DMA(shape)
    smem = pl.BlockSpec(memory_space=pltpu.SMEM)
    vmem = pl.BlockSpec(memory_space=pltpu.VMEM)
    anywhere = pl.BlockSpec(memory_space=pl.ANY)
    lout, gx, gwin, gwout = pl.pallas_call(
        kernel,
        out_shape=(
            jax.ShapeDtypeStruct((2 * BLK, WIDTH), BF16),
            jax.ShapeDtypeStruct((2, BLK, WIDTH), BF16),
            jax.ShapeDtypeStruct((WIDTH, HID), BF16),
            jax.ShapeDtypeStruct((HID, WIDTH), BF16),
        ),
        in_specs=[smem, smem, vmem] + [anywhere] * 4,
        out_specs=(vmem, vmem, vmem, vmem),
        scratch_shapes=[
            vm(SLOTS, BLK, BLK), vm(SLOTS, BLK, BLK), vm(WIDTH, HID), vm(HID, WIDTH),
            vm(2 * BLK, WIDTH),
            vm(BLOCKS, BLK, WIDTH), vm(BLOCKS, BLK, WIDTH), vm(SLOTS + 1, BLK, WIDTH, t=F32),
            vm(8, 2, BLK, WIDTH), vm(8, 2, BLK, WIDTH), vm(8, 2, BLK, WIDTH),
            vm(8, 2, BLK, WIDTH), vm(2, BLK, WIDTH, t=F32),
            vm(2, 4, 2, 2, BLK, WIDTH), vm(2, 4, 2, 2, BLK, WIDTH),
            vm(2, BLK, WIDTH), vm(2, BLK, WIDTH), vm(2, BLK, WIDTH),
            vm(4096, 128, t=F32), vm(8, 256, 128), vm(8, 256, 128), vm(8, 256, 128),
            vm(8, 256, 128), vm(256, 128, t=F32), vm(16, 16, 128), vm(16, 16, 128),
            vm(16, 128), vm(4096, 128),
            dma(4), dma(2, 4, 2), dma(2, 4, 2), dma(2), dma(2), dma(8), dma(8), dma(8), dma(8),
            dma(8), dma(8), dma(8), dma(8), dma(2, 4, 2), dma(2, 4, 2), dma(1), dma(1),
            dma(8), dma(8), dma(16), dma(16), dma(16), dma(16), dma(8), dma(8), dma(8), dma(8),
        ],
        compiler_params=pltpu.CompilerParams(
            collective_id=0, has_side_effects=True, vmem_limit_bytes=52 * 2**20
        ),
        name="layer",
    )(
        tab, block_count[0], features.reshape(2, BLK, WIDTH), block_values[0, 0],
        weight_in, weight_out, cot,
    )
    return lout, gx.reshape(2 * BLK, WIDTH), gwin.astype(F32), gwout.astype(F32)


def solution(mesh):
    return jax.shard_map(
        body,
        mesh=mesh,
        in_specs=(
            P(("col", "row"), None),
            P("row", "col", None, None, None),
            P("row", "col", None),
            P("row", "col", None),
            P("row", "col"),
            P(),
            P(),
            P(("row", "col"), None),
        ),
        out_specs=(P(("row", "col"), None), P(("col", "row"), None), P(), P()),
        check_vma=False,
    )
```

time: 739 us -> 113 us (0.15)
  waiting for transfers between devices: 655 us -> 0 us
  Pallas kernels: 0 us -> 104 us
  local copies, waits for them, and re-layouts: 28.1 us -> 3.76 us
  other arithmetic: 23.6 us -> 2.39 us
  matrix products: 16.3 us -> 0 us
  between operations: 14.5 us -> 1.33 us
    psum x1 -> x0, waiting for transfers between devices: 266 us -> none  [body(): grad_w_in, grad_w_out = lax.psum((local_w_in, local_w_out), ('row', 'col'))]
    reduce_scatter x2 -> x0, waiting for transfers between devices: 265 us -> none  [the longest x1 201 us: body(): lax.psum_scatter(partial_back, 'row', scatter_dimension=0, tiled=True)]
    all_gather x2 -> x0, waiting for transfers between devices: 123 us -> none  [the longest x1 87.6 us: body(): gathered = lax.all_gather(features, 'row', axis=0, tiled=True)]
    pallas_call x0 -> x1, Pallas kernels: none -> 104 us  [body(): pl.pallas_call(kernel, out_shape=(jax.ShapeDtypeStruct((2 * BLK, WIDTH),...]
    scatter-add x2 -> x0, other arithmetic: 20 us -> none  [aggregate(): jax.ops.segment_sum(prod, placed, num_segments=out_blocks)]
    dot_general x8 -> x0, matrix products: 16.3 us -> none  [the longest x1 2.93 us: aggregate(): jnp.einsum('sij,sjf->sif', values, taken, preferred_element_type=jnp.floa...]
    mul x2 -> x0, local copies, waits for them, and re-layouts: 11.2 us -> none  [aggregate(): prod = prod * (live_mask * inside)[:, None, None]]
  transfers between devices with their start and end apart: 5 -> 0, of which waited for: 5 -> 0; matrix products, arithmetic and copies ran while one was open for 1% -> 0% of each run, Pallas kernels for 0% -> 0%
where the time goes in v1:
time: 113 us; the launch traced here: 112 us
  Pallas kernels  104 us (92%)
  local copies, waits for them, and re-layouts  3.76 us (3%)
  other arithmetic  2.39 us (2%)
  between operations  1.33 us (1%)
    pallas_call x1, Pallas kernels, body(): pl.pallas_call(kernel, out_shape=(jax.ShapeDtypeStruct((2 * BLK, WIDTH),...  104 us
    unnamed x10, local copies, waits for them, and re-layouts  3.76 us

profile of v1, /device:TPU:2, one launch (start us, length us, event | category | flops | bytes accessed | tf_op | source)
XLA Modules:
  0.0 111.6 jit_solution(16254235944103654376)
XLA Ops:
  1.3 0.0 copy-start.2
  1.3 0.0 copy-start.3
  1.3 0.6 copy-done.2
  1.9 0.0 copy-done.3
  2.0 0.2 select_reduce_fusion.1
  2.2 0.0 copy-start
  2.2 0.9 copy-done
  3.1 0.0 copy-start.1
  3.1 0.9 copy-done.1
  4.0 104.1 %layer.1 = (bf16[256,256]{1,0:T(8,128)(2,1)S(1)}, bf16[2,128,256]{2,1,0:T(8,128)(2,1)S(1)}, bf16[256,1024]{1,0:T(8,128)(2,1)S(1)}, bf16[1024,256]{1,0:T(8,128)(2,1)S(1)}) custom-call(s32[6,32]{1,0:T(8,128)S(1)} %pad_add_fusion.tab, s32[1]{0:T(128)} %bitcast.6.count, bf16[2,128,256]{2,1,0:T(8,128)(2,1)S(1)} %bitcast.8, bf16[32,128,128]{2,1,0:T(8,128)(2,1)} %bitcast.9, ...), custom_call_target="tpu_custom_call" | custom-call | tf_op jit(solution)/shard_map/layer/pallas_call | solution.py:372
  108.2 1.1 convert_element_type.6
  109.3 1.0 convert_element_type.7
  110.3 0.7 copy.15
  111.0 0.7 copy.16
  (4 shorter events, 0.0 us)
Async XLA Ops:
  1.3 0.7 copy-start.2
  1.3 0.7 copy-start.3
  2.2 0.9 copy-start
  3.1 0.9 copy-start.1
